TPU v7x, 32 devices: a whole 2x2x4 slice. The times are simulated.
32 devices in a mesh: groups: 2 (over y), rows: 4 (over z), disp: 2 (over x), cols: 2 (over core).
Axes of the slice: x: 2, y: 2, z: 4, core: 2. Of those that a mesh axis runs over, the one named last changes fastest.
Arguments:
- cost_volume_section: bfloat16 [32, 32, 8192], P(('groups', 'rows'), 'cols', 'disp'), parts along dimension 0, may hold values from -6 to 6
- picture_convolution_taps_grid: bfloat16 [3, 3, 3, 64, 64], replicated, may hold values from -0.25 to 0.25
- picture_convolution_offset_terms: float32 [3, 64], replicated, may hold values from -3 to 3
- shiftaxis_convolution_taps: bfloat16 [2, 17, 64, 64], replicated, may hold values from -0.1875 to 0.1875
- shiftaxis_convolution_biases: float32 [2, 64], replicated, may hold values from -3 to 3
- prior_norm_scale: float32 [64], replicated, may hold values from 0.1 to 1.9
- qkv_side_projections: bfloat16 [64, 192], replicated, may hold values from -0.75 to 0.75
- attn_exit_projection: bfloat16 [64, 64], replicated, may hold values from -0.75 to 0.75
- each_mixer_scale: float32 [4], replicated, may hold values from 0.25 to 25, as said below
- gating_projection: bfloat16 [64, 64], replicated, may hold values from -0.75 to 0.75
- gating_offset_terms: float32 [64], replicated, may hold values from -3 to 3
Outputs:
- filtered: bfloat16 [32, 32, 8192], P(('groups', 'rows'), 'cols', 'disp'), parts along dimension 0
There are 2 independent parts, one for each index of `groups`. A program takes and returns all parts, laid end to end along the dimension named above; an argument that names none is the same for every part. Nothing has to cross between parts.
Inputs may be any that keep to these rules, and one draw needn't show every extreme that they name: `each_mixer_scale`: positive score scales, one for each head.
All inputs are finite; a program needn't handle non-finite values.
Results may differ from a plain program's by a relative error of at most 0.0095.
Values may be sent and summed in bfloat16 or wider, within the bound.
A program may use at most 64 MiB of HBM per device.

v0:
```python
import functools
import math

import jax
import jax.numpy as jnp
from jax import lax
from jax.experimental import pallas as pl
from jax.experimental.pallas import tpu as pltpu
from jax.sharding import PartitionSpec as P

MESH = pl.DeviceIdType.MESH
BF16 = jnp.bfloat16
F32 = jnp.float32
LANES = 256
DIRECTIONS = [(dy, dx) for dy in (-1, 0, 1) for dx in (-1, 0, 1) if (dy, dx) != (0, 0)]


def sigmoid(v):
    return 0.5 * jnp.tanh(0.5 * v) + 0.5


def dot(a, b):
    return jnp.dot(a, b, preferred_element_type=F32)


def kernel(
    sizes,
    x_ref,
    plane_taps,
    plane_bias,
    shift_taps,
    shift_bias,
    gain_ref,
    qkv_ref,
    exit_ref,
    scale_ref,
    gate_ref,
    gate_bias,
    out_ref,
    fields,
    slabs,
    lines,
    padded,
    second,
    joined,
    mixed,
    back,
    returned,
    stage,
    w_plane,
    w_shift,
    w_qkv,
    w_exit,
    w_gate,
    halo_send,
    halo_recv,
    there_send,
    there_recv,
    back_send,
    back_recv,
):
    nr, nd, nc, H, W, bl, C, layers, taps, heads = sizes
    pack = LANES // C
    B = nd * bl
    half = taps // 2
    reach = (half + pack - 1) // pack
    hr = H // nd
    px = hr * W
    row, disp, col = lax.axis_index("rows"), lax.axis_index("disp"), lax.axis_index("cols")

    def exists(dy, dx):
        ok = None
        for d, at, n in ((dy, row, nr), (dx, col, nc)):
            if d == -1:
                c = at > 0
            elif d == 1:
                c = at < n - 1
            else:
                continue
            ok = c if ok is None else jnp.logical_and(ok, c)
        return ok

    barrier = pltpu.get_barrier_semaphore()
    expected = jnp.int32(nd - 1)
    for dy, dx in DIRECTIONS:
        here = exists(dy, dx)
        expected = expected + here.astype(jnp.int32)

        @pl.when(here)
        def _():
            pl.semaphore_signal(
                barrier, inc=1, device_id={"rows": row + dy, "cols": col + dx}, device_id_type=MESH
            )

    for o in range(1, nd):
        pl.semaphore_signal(
            barrier, inc=1, device_id={"disp": lax.rem(disp + o, nd)}, device_id_type=MESH
        )

    for h in range(H):
        for b in range(bl):
            block = x_ref[h, :, b * LANES : (b + 1) * LANES].astype(F32)
            for s in range(2):
                stage[s, h * bl * W + b * W : h * bl * W + (b + 1) * W, :] = block[
                    :, s * 128 : (s + 1) * 128
                ]
    for h in range(H):
        for w in range(W):
            for s in range(2):
                fields[0, 1 + h, 1 + w, :, s * 128 : (s + 1) * 128] = stage[
                    s, pl.ds(h * bl * W + w, bl, stride=W), :
                ].astype(BF16)

    pl.semaphore_wait(barrier, expected)

    def span(d, n):
        return slice(1, n + 1) if d == 0 else (slice(1, 2) if d == -1 else slice(n, n + 1))

    def landing(d, n):
        return slice(1, n + 1) if d == 0 else (slice(n + 1, n + 2) if d == -1 else slice(0, 1))

    def halo_copy(k, i):
        dy, dx = DIRECTIONS[i]
        return pltpu.make_async_remote_copy(
            src_ref=fields.at[k, span(dy, H), span(dx, W)],
            dst_ref=fields.at[k, landing(dy, H), landing(dx, W)],
            send_sem=halo_send.at[k, i],
            recv_sem=halo_recv.at[k, i],
            device_id={"rows": row + dy, "cols": col + dx},
            device_id_type=MESH,
        )

    order = sorted(range(8), key=lambda i: DIRECTIONS[i][1] != 0)

    def halo_start(k):
        for i in order:
            @pl.when(exists(*DIRECTIONS[i]))
            def _():
                halo_copy(k, i).start()

    def halo_wait(k, which):
        for i in which:
            dy, dx = DIRECTIONS[i]

            @pl.when(exists(-dy, -dx))
            def _():
                halo_copy(k, i).wait_recv()

    halo_start(0)

    for i in range(8):
        dy, dx = DIRECTIONS[i]

        @pl.when(jnp.logical_not(exists(-dy, -dx)))
        def _():
            for k in range(layers):
                view = fields.at[k, landing(dy, H), landing(dx, W)]
                view[...] = jnp.zeros(view.shape, BF16)

    r_at = lax.broadcasted_iota(jnp.int32, (C, LANES), 0)
    l_at = lax.broadcasted_iota(jnp.int32, (C, LANES), 1)
    repeat = (l_at % C == r_at).astype(BF16)
    group = l_at // C

    def spread(w):
        return dot(w, repeat)

    for l in range(layers):
        for t in range(9):
            wide = spread(plane_taps[(l * 9 + t) * C : (l * 9 + t + 1) * C, :])
            for i in range(pack):
                at = t * LANES + i * C
                w_plane[l, at : at + C, :] = jnp.where(group == i, wide, 0.0).astype(BF16)

    bias_p = jnp.concatenate([plane_bias[...]] * pack, axis=1)
    bias_s = jnp.concatenate([shift_bias[...]] * pack, axis=1)
    bias_g = jnp.concatenate([gate_bias[...]] * pack, axis=1)
    gain = jnp.concatenate([gain_ref[...]] * pack, axis=1)

    def late_weights():
        for l in range(2):
            wides = [
                spread(shift_taps[(l * taps + t) * C : (l * taps + t + 1) * C, :])
                for t in range(taps)
            ]
            for j in range(-reach, reach + 1):
                for i in range(pack):
                    value = jnp.zeros((C, LANES), F32)
                    for o in range(pack):
                        t = pack * j + i - o + half
                        if 0 <= t < taps:
                            value = jnp.where(group == o, wides[t], value)
                    at = (j + reach) * LANES + i * C
                    w_shift[l, at : at + C, :] = value.astype(BF16)
        a = lax.broadcasted_iota(jnp.int32, (3 * C, 3 * 128), 0)
        b = lax.broadcasted_iota(jnp.int32, (3 * C, 3 * 128), 1)
        place = jnp.logical_and(a // C == b // 128, a % C == b % 128).astype(BF16)
        wide = dot(qkv_ref[...], place).astype(BF16)
        w_qkv[...] = jnp.zeros(w_qkv.shape, BF16)
        for i in range(pack):
            w_qkv[i * C : (i + 1) * C, i * 384 : (i + 1) * 384] = wide
        w_exit[...] = jnp.zeros(w_exit.shape, BF16)
        wide = spread(exit_ref[...])
        for i in range(pack):
            w_exit[i * 128 : i * 128 + C, :] = jnp.where(group == i, wide, 0.0).astype(BF16)
        wide = spread(gate_ref[...])
        for i in range(pack):
            w_gate[i * C : (i + 1) * C, :] = jnp.where(group == i, wide, 0.0).astype(BF16)
        padded[:, 0:8, :] = jnp.zeros((px, 8, LANES), F32)
        padded[:, B + 8 : B + 16, :] = jnp.zeros((px, 8, LANES), F32)

    def there_copy(o):
        to = lax.rem(disp + o, nd)
        return pltpu.make_async_remote_copy(
            src_ref=slabs.at[to],
            dst_ref=lines.at[disp],
            send_sem=there_send.at[o - 1],
            recv_sem=there_recv.at[o - 1],
            device_id={"disp": to},
            device_id_type=MESH,
        )

    def plane_row(k, h):
        lhs = jnp.concatenate(
            [
                fields[k, h + dy, dx : dx + W].reshape(W * bl, LANES)
                for dy in range(3)
                for dx in range(3)
            ],
            axis=1,
        )
        v = dot(lhs, w_plane[k]) + bias_p[k : k + 1]
        v = (v * sigmoid(v)).astype(BF16).reshape(W, bl, LANES)
        if k + 1 < layers:
            fields[k + 1, 1 + h, 1 : W + 1] = v
        else:
            slabs[h // hr, (h % hr) * W : (h % hr + 1) * W] = v

    sides = [i for i in range(8) if DIRECTIONS[i][0] == 0]
    others = [i for i in range(8) if DIRECTIONS[i][0] != 0]
    for k in range(layers):
        halo_wait(k, sides)
        for h in range(1, H - 1):
            plane_row(k, h)
        if k == 0:
            late_weights()
        halo_wait(k, others)
        for h in (0, H - 1):
            plane_row(k, h)
        if k + 1 < layers:
            halo_start(k + 1)

    for o in range(1, nd):
        there_copy(o).start()
    lines[disp] = slabs[disp]
    for o in range(1, nd):
        there_copy(o).wait_recv()

    for s in range(nd):
        padded[:, 8 + s * bl : 8 + (s + 1) * bl, :] = lines[s].astype(F32)
    step = 8 if px % 8 == 0 else px

    def shift_conv(l, p0):
        lhs = jnp.concatenate(
            [
                padded[pl.ds(p0, step), 8 + j : 8 + j + B, :].astype(BF16).reshape(step * B, LANES)
                for j in range(-reach, reach + 1)
            ],
            axis=1,
        )
        return dot(lhs, w_shift[l]) + bias_s[l : l + 1]

    ones_a = lax.broadcasted_iota(jnp.int32, (LANES, LANES), 0) // C
    ones_b = lax.broadcasted_iota(jnp.int32, (LANES, LANES), 1) // C
    ones = (ones_a == ones_b).astype(BF16)

    def conv_chunk(c, carry):
        p0 = c * step
        v = shift_conv(0, p0)
        v = (v * sigmoid(v)).astype(BF16).astype(F32)
        padded[pl.ds(p0, step), 8 : 8 + B, :] = v.reshape(step, B, LANES)
        v = shift_conv(1, p0).astype(BF16)
        second[pl.ds(p0, step)] = v.reshape(step, B, LANES)
        v = v.astype(F32)
        square = v * v
        high = square.astype(BF16)
        low = (square - high.astype(F32)).astype(BF16)
        mean = (dot(high, ones) + dot(low, ones)) * (1.0 / C)
        normed = (v * lax.rsqrt(mean + 1e-05) * gain).astype(BF16)
        joined[pl.ds(p0, step)] = dot(normed, w_qkv[...]).astype(BF16).reshape(step, B, pack * 384)
        return carry

    lax.fori_loop(0, px // step, conv_chunk, 0)

    D = pack * B
    hd = C // heads
    lane = lax.broadcasted_iota(jnp.int32, (D, 128), 1)
    srow = lax.broadcasted_iota(jnp.int32, (128, D), 0)
    factor = math.log2(math.e) / math.sqrt(hd)

    def one_pixel(p):
        t = joined[p]
        q, k, v = (
            jnp.concatenate(
                [t[:, i * 384 + g * 128 : i * 384 + (g + 1) * 128] for i in range(pack)], axis=0
            )
            for g in range(3)
        )
        keys = jnp.concatenate(
            [jnp.where(lane // hd == h, k, jnp.zeros_like(k)) for h in range(heads)], axis=0
        )
        scores = lax.dot_general(keys, q, (((1,), (1,)), ((), ())), preferred_element_type=F32)
        weights = []
        for h in range(heads):
            part = scores[h * D : (h + 1) * D]
            top = jnp.max(part, axis=0, keepdims=True)
            weights.append(jnp.exp2((part - top) * (scale_ref[h] * factor)).astype(BF16))
        weights = jnp.concatenate(weights, axis=0)
        vt = v.astype(F32).T
        values = jnp.concatenate(
            [
                jnp.where(
                    srow // hd == h, vt, jnp.where((srow - C) // hd == h, 1.0, 0.0)
                ).astype(BF16)
                for h in range(heads)
            ],
            axis=1,
        )
        o = dot(values, weights)
        o = o[:C] / o[C : 2 * C]
        if C < 128:
            o = jnp.concatenate([o, jnp.zeros((128 - C, D), F32)], axis=0)
        o = o.T.astype(BF16)
        for i in range(pack):
            mixed[p, :, i * 128 : (i + 1) * 128] = o[i * B : (i + 1) * B]

    group_px = 4 if px % 4 == 0 else 1

    def pixels(c, carry):
        for i in range(group_px):
            one_pixel(c * group_px + i)
        return carry

    lax.fori_loop(0, px // group_px, pixels, 0)

    def exit_chunk(c, carry):
        p0 = c * step
        v = second[pl.ds(p0, step)].astype(F32).reshape(step * B, LANES)
        v = v + dot(mixed[pl.ds(p0, step)].reshape(step * B, pack * 128), w_exit[...])
        v = v.astype(BF16).reshape(step, B, LANES)
        for s in range(nd):
            back[s, pl.ds(p0, step)] = v[:, s * bl : (s + 1) * bl]
        return carry

    lax.fori_loop(0, px // step, exit_chunk, 0)

    def back_copy(o):
        to = lax.rem(disp + o, nd)
        return pltpu.make_async_remote_copy(
            src_ref=back.at[to],
            dst_ref=returned.at[disp],
            send_sem=back_send.at[o - 1],
            recv_sem=back_recv.at[o - 1],
            device_id={"disp": to},
            device_id_type=MESH,
        )

    for o in range(1, nd):
        back_copy(o).start()
    returned[disp] = back[disp]
    for o in range(1, nd):
        back_copy(o).wait_recv()

    for h in range(H):
        v = returned[h // hr, (h % hr) * W : (h % hr + 1) * W].reshape(W * bl, LANES)
        v = sigmoid(dot(v, w_gate[...]) + bias_g)
        v = v * fields[0, 1 + h, 1 : W + 1].astype(F32).reshape(W * bl, LANES)
        for s in range(2):
            stage[s, h * W * bl : (h + 1) * W * bl, :] = v[:, s * 128 : (s + 1) * 128]
    for h in range(H):
        for b in range(bl):
            for s in range(2):
                out_ref[h, :, b * LANES + s * 128 : b * LANES + (s + 1) * 128] = stage[
                    s, pl.ds(h * W * bl + b, W, stride=bl), :
                ].astype(BF16)

    for k in range(layers):
        for i in range(8):
            @pl.when(exists(*DIRECTIONS[i]))
            def _():
                halo_copy(k, i).wait_send()
    for o in range(1, nd):
        there_copy(o).wait_send()
        back_copy(o).wait_send()


def per_device(axes, x, ptaps, pbias, staps, sbias, gain, qkv, wexit, scale, gate, gbias):
    nr, nd, nc = axes
    H, W, flat = x.shape
    C = ptaps.shape[-1]
    layers, taps, heads = ptaps.shape[0], staps.shape[1], scale.shape[0]
    pack = LANES // C
    bl = flat // LANES
    B = nd * bl
    px = H * W // nd
    reach = (taps // 2 + pack - 1) // pack
    sizes = (nr, nd, nc, H, W, bl, C, layers, taps, heads)
    vmem = pl.BlockSpec(memory_space=pltpu.VMEM)
    specs = [vmem] * 11
    specs[8] = pl.BlockSpec(memory_space=pltpu.SMEM)
    peers = max(nd - 1, 1)
    return pl.pallas_call(
        functools.partial(kernel, sizes),
        out_shape=jax.ShapeDtypeStruct(x.shape, x.dtype),
        in_specs=specs,
        out_specs=vmem,
        scratch_shapes=[
            pltpu.VMEM((layers, H + 2, W + 2, bl, LANES), BF16),
            pltpu.VMEM((nd, px, bl, LANES), BF16),
            pltpu.VMEM((nd, px, bl, LANES), BF16),
            pltpu.VMEM((px, B + 16, LANES), F32),
            pltpu.VMEM((px, B, LANES), BF16),
            pltpu.VMEM((px, B, pack * 384), BF16),
            pltpu.VMEM((px, B, pack * 128), BF16),
            pltpu.VMEM((nd, px, bl, LANES), BF16),
            pltpu.VMEM((nd, px, bl, LANES), BF16),
            pltpu.VMEM((2, H * W * bl, 128), F32),
            pltpu.VMEM((layers, 9 * LANES, LANES), BF16),
            pltpu.VMEM((2, (2 * reach + 1) * LANES, LANES), BF16),
            pltpu.VMEM((LANES, pack * 384), BF16),
            pltpu.VMEM((pack * 128, LANES), BF16),
            pltpu.VMEM((LANES, LANES), BF16),
            pltpu.SemaphoreType.DMA((layers, 8)),
            pltpu.SemaphoreType.DMA((layers, 8)),
            pltpu.SemaphoreType.DMA((peers,)),
            pltpu.SemaphoreType.DMA((peers,)),
            pltpu.SemaphoreType.DMA((peers,)),
            pltpu.SemaphoreType.DMA((peers,)),
        ],
        compiler_params=pltpu.CompilerParams(
            collective_id=0, has_side_effects=True, vmem_limit_bytes=48 * 1024 * 1024
        ),
    )(
        x,
        ptaps.reshape(-1, C),
        pbias,
        staps.reshape(-1, C),
        sbias,
        gain.reshape(1, C),
        qkv,
        wexit,
        scale,
        gate,
        gbias.reshape(1, C),
    )


def solution(mesh):
    axes = tuple(mesh.shape[a] for a in ("rows", "disp", "cols"))
    spec = P(("groups", "rows"), "cols", "disp")
    return jax.shard_map(
        functools.partial(per_device, axes),
        mesh=mesh,
        in_specs=(spec,) + (P(),) * 10,
        out_specs=spec,
        check_vma=False,
    )
```

profile of v0, /device:TPU:0, one launch (start us, length us, event | category | flops | bytes accessed | tf_op | source)
XLA Modules:
  0.0 58.7 jit_solution(10233095089181432037)
XLA Ops:
  0.0 0.0 copy-start.9
  0.0 0.0 copy-start.10
  0.0 0.0 copy-start.6
  0.0 0.0 copy-start.7
  0.0 0.0 copy-start.8
  0.0 0.6 %copy-done.9 = f32[4]{0:T(128)S(1)} copy-done((f32[4]{0:T(128)S(1)}, f32[4]{0:T(128)}, u32[]{:S(2)}) %copy-start.9) | copy-done | bytes 40
  0.7 0.0 copy-done.10
  0.7 0.0 copy-done.6
  0.7 0.0 copy-done.7
  0.7 0.0 copy-done.8
  0.7 0.0 copy-start
  0.7 1.1 %copy-done = bf16[2,17,64,64]{3,2,1,0:T(8,128)(2,1)S(1)} copy-done((bf16[2,17,64,64]{3,2,1,0:T(8,128)(2,1)S(1)}, bf16[2,17,64,64]{3,2,1,0:T(8,128)(2,1)}, u32[]{:S(2)}) %copy-start) | copy-done | bytes 278552
  1.8 0.0 copy-start.1
  1.8 1.0 %copy-done.1 = bf16[4,16,4096]{2,1,0:T(8,128)(2,1)S(1)} copy-done((bf16[4,16,4096]{2,1,0:T(8,128)(2,1)S(1)}, bf16[4,16,4096]{2,1,0:T(8,128)(2,1)}, u32[]{:S(2)}) %copy-start.1) | copy-done | bytes 524312
  2.8 0.0 copy-start.2
  2.8 1.0 %copy-done.2 = bf16[3,3,3,64,64]{4,3,2,1,0:T(8,128)(2,1)S(1)} copy-done((bf16[3,3,3,64,64]{4,3,2,1,0:T(8,128)(2,1)S(1)}, bf16[3,3,3,64,64]{4,3,2,1,0:T(8,128)(2,1)}, u32[]{:S(2)}) %copy-start.2) | copy-done | bytes 221208
  3.8 0.0 copy-start.3
  3.8 0.8 %copy-done.3 = bf16[64,192]{1,0:T(8,128)(2,1)S(1)} copy-done((bf16[64,192]{1,0:T(8,128)(2,1)S(1)}, bf16[64,192]{1,0:T(8,128)(2,1)}, u32[]{:S(2)}) %copy-start.3) | copy-done | bytes 24600
  4.6 0.0 copy-start.4
  4.6 0.7 %copy-done.4 = bf16[64,64]{1,0:T(8,128)(2,1)S(1)} copy-done((bf16[64,64]{1,0:T(8,128)(2,1)S(1)}, bf16[64,64]{1,0:T(8,128)(2,1)}, u32[]{:S(2)}) %copy-start.4) | copy-done | bytes 8216
  5.3 0.0 copy-start.5
  5.3 0.7 %copy-done.5 = bf16[64,64]{1,0:T(8,128)(2,1)S(1)} copy-done((bf16[64,64]{1,0:T(8,128)(2,1)S(1)}, bf16[64,64]{1,0:T(8,128)(2,1)}, u32[]{:S(2)}) %copy-start.5) | copy-done | bytes 8216
  6.0 51.8 %shard_map.109 = bf16[4,16,4096]{2,1,0:T(8,128)(2,1)S(1)} custom-call(bf16[4,16,4096]{2,1,0:T(8,128)(2,1)S(1)} %copy-done.1, bf16[1728,64]{1,0:T(8,128)(2,1)S(1)} %bitcast.5, f32[3,64]{1,0:T(4,128)S(1)} %copy-done.6, bf16[2176,64]{1,0:T(8,128)(2,1)S(1)} %bitcast.4, f32[2,64]{1,0:T(2,128)S(1)} %copy-done.7, f32[1,64]{1,0:T(1,128)S(1)} %bitcast.6, ...), custom_call_target="tpu_custom_call" | custom-call | tf_op jit(solution)/shard_map/pallas_call | solution.py:412
  57.9 0.8 %copy.13 = bf16[4,16,4096]{2,1,0:T(8,128)(2,1)} copy(bf16[4,16,4096]{2,1,0:T(8,128)(2,1)S(1)} %shard_map.109) | data formatting | bytes 1048576
Async XLA Ops:
  0.0 0.7 %copy-start.9 = (f32[4]{0:T(128)S(1)}, f32[4]{0:T(128)}, u32[]{:S(2)}) copy-start(f32[4]{0:T(128)} %scale_ref.1) | copy-start | bytes 52
  0.0 0.7 %copy-start.10 = (f32[64]{0:T(128)S(1)}, f32[64]{0:T(128)}, u32[]{:S(2)}) copy-start(f32[64]{0:T(128)} %param.21) | copy-start | bytes 772
  0.0 0.7 %copy-start.6 = (f32[3,64]{1,0:T(4,128)S(1)}, f32[3,64]{1,0:T(4,128)}, u32[]{:S(2)}) copy-start(f32[3,64]{1,0:T(4,128)} %plane_bias.1) | copy-start | bytes 2308
  0.0 0.7 %copy-start.7 = (f32[2,64]{1,0:T(2,128)S(1)}, f32[2,64]{1,0:T(2,128)}, u32[]{:S(2)}) copy-start(f32[2,64]{1,0:T(2,128)} %shift_bias.1) | copy-start | bytes 1540
  0.0 0.7 %copy-start.8 = (f32[64]{0:T(128)S(1)}, f32[64]{0:T(128)}, u32[]{:S(2)}) copy-start(f32[64]{0:T(128)} %param.16) | copy-start | bytes 772
  0.7 1.1 %copy-start = (bf16[2,17,64,64]{3,2,1,0:T(8,128)(2,1)S(1)}, bf16[2,17,64,64]{3,2,1,0:T(8,128)(2,1)}, u32[]{:S(2)}) copy-start(bf16[2,17,64,64]{3,2,1,0:T(8,128)(2,1)} %param.14) | copy-start | bytes 835588
  1.8 1.0 %copy-start.1 = (bf16[4,16,4096]{2,1,0:T(8,128)(2,1)S(1)}, bf16[4,16,4096]{2,1,0:T(8,128)(2,1)}, u32[]{:S(2)}) copy-start(bf16[4,16,4096]{2,1,0:T(8,128)(2,1)} %x_ref.1) | copy-start | bytes 1572868
  2.8 1.0 %copy-start.2 = (bf16[3,3,3,64,64]{4,3,2,1,0:T(8,128)(2,1)S(1)}, bf16[3,3,3,64,64]{4,3,2,1,0:T(8,128)(2,1)}, u32[]{:S(2)}) copy-start(bf16[3,3,3,64,64]{4,3,2,1,0:T(8,128)(2,1)} %param.12) | copy-start | bytes 663556
  3.8 0.8 %copy-start.3 = (bf16[64,192]{1,0:T(8,128)(2,1)S(1)}, bf16[64,192]{1,0:T(8,128)(2,1)}, u32[]{:S(2)}) copy-start(bf16[64,192]{1,0:T(8,128)(2,1)} %qkv_ref.1) | copy-start | bytes 73732
  4.6 0.7 %copy-start.4 = (bf16[64,64]{1,0:T(8,128)(2,1)S(1)}, bf16[64,64]{1,0:T(8,128)(2,1)}, u32[]{:S(2)}) copy-start(bf16[64,64]{1,0:T(8,128)(2,1)} %exit_ref.1) | copy-start | bytes 24580
  5.3 0.7 %copy-start.5 = (bf16[64,64]{1,0:T(8,128)(2,1)S(1)}, bf16[64,64]{1,0:T(8,128)(2,1)}, u32[]{:S(2)}) copy-start(bf16[64,64]{1,0:T(8,128)(2,1)} %gate_ref.1) | copy-start | bytes 24580
where the time goes:
time: 59.1 us; the launch traced here: 58.7 us
  Pallas kernels  51.8 us (88%)
  local copies, waits for them, and re-layouts  6.81 us (12%)
    pallas_call x1, Pallas kernels, per_device(): pl.pallas_call(functools.partial(kernel, sizes), out_shape=jax.ShapeDtype...  51.8 us
    unnamed x23, local copies, waits for them, and re-layouts  6.81 us

commit v1 on v0

v1 whole, which is shorter than its diff:
```python
import functools
import math

import jax
import jax.numpy as jnp
from jax import lax
from jax.experimental import pallas as pl
from jax.experimental.pallas import tpu as pltpu
from jax.sharding import PartitionSpec as P

MESH = pl.DeviceIdType.MESH
BF16 = jnp.bfloat16
F32 = jnp.float32
LANES = 256
DIRECTIONS = [(dy, dx) for dy in (-1, 0, 1) for dx in (-1, 0, 1) if (dy, dx) != (0, 0)]


def sigmoid(v):
    return 0.5 * jnp.tanh(0.5 * v) + 0.5


def dot(a, b):
    return jnp.dot(a, b, preferred_element_type=F32)


def kernel(
    sizes,
    *refs,
):
    sources, out_ref, held, refs = refs[:11], refs[11], refs[12:23], refs[23:]
    (
        x_ref,
        plane_taps,
        plane_bias,
        shift_taps,
        shift_bias,
        gain_ref,
        qkv_ref,
        exit_ref,
        scale_ref,
        gate_ref,
        gate_bias,
    ) = held
    (
        fields,
        slabs,
        lines,
        padded,
        second,
        joined,
        mixed,
        back,
        returned,
        stage,
        w_plane,
        w_shift,
        w_qkv,
        w_exit,
        w_gate,
        halo_send,
        halo_recv,
        there_send,
        there_recv,
        back_send,
        back_recv,
        load,
    ) = refs
    nr, nd, nc, H, W, bl, C, layers, taps, heads = sizes
    pack = LANES // C
    B = nd * bl
    half = taps // 2
    reach = (half + pack - 1) // pack
    hr = H // nd
    step = 8 if W % 8 == 0 else W
    parts = W // step
    seq = list(range(1, H - 1)) + sorted({0, H - 1})
    stages = [seq[a * nd : (a + 1) * nd] for a in range(hr)]
    row, disp, col = lax.axis_index("rows"), lax.axis_index("disp"), lax.axis_index("cols")

    def exists(dy, dx):
        ok = None
        for d, at, n in ((dy, row, nr), (dx, col, nc)):
            if d == -1:
                c = at > 0
            elif d == 1:
                c = at < n - 1
            else:
                continue
            ok = c if ok is None else jnp.logical_and(ok, c)
        return ok

    loads = [pltpu.make_async_copy(a, b, load.at[i]) for i, (a, b) in enumerate(zip(sources, held))]
    for c in loads:
        c.start()

    barrier = pltpu.get_barrier_semaphore()
    expected = jnp.int32(nd - 1)
    for dy, dx in DIRECTIONS:
        here = exists(dy, dx)
        expected = expected + here.astype(jnp.int32)

        @pl.when(here)
        def _():
            pl.semaphore_signal(
                barrier, inc=1, device_id={"rows": row + dy, "cols": col + dx}, device_id_type=MESH
            )

    for o in range(1, nd):
        pl.semaphore_signal(
            barrier, inc=1, device_id={"disp": lax.rem(disp + o, nd)}, device_id_type=MESH
        )

    loads[0].wait()
    for h in range(H):
        for b in range(bl):
            block = x_ref[h, :, b * LANES : (b + 1) * LANES].astype(F32)
            for s in range(2):
                stage[s, h * bl * W + b * W : h * bl * W + (b + 1) * W, :] = block[
                    :, s * 128 : (s + 1) * 128
                ]
    for h in range(H):
        for w in range(W):
            for s in range(2):
                fields[0, 1 + h, 1 + w, :, s * 128 : (s + 1) * 128] = stage[
                    s, pl.ds(h * bl * W + w, bl, stride=W), :
                ].astype(BF16)

    pl.semaphore_wait(barrier, expected)

    def span(d, n):
        return slice(1, n + 1) if d == 0 else (slice(1, 2) if d == -1 else slice(n, n + 1))

    def landing(d, n):
        return slice(1, n + 1) if d == 0 else (slice(n + 1, n + 2) if d == -1 else slice(0, 1))

    def halo_copy(k, i):
        dy, dx = DIRECTIONS[i]
        return pltpu.make_async_remote_copy(
            src_ref=fields.at[k, span(dy, H), span(dx, W)],
            dst_ref=fields.at[k, landing(dy, H), landing(dx, W)],
            send_sem=halo_send.at[k, i],
            recv_sem=halo_recv.at[k, i],
            device_id={"rows": row + dy, "cols": col + dx},
            device_id_type=MESH,
        )

    order = sorted(range(8), key=lambda i: DIRECTIONS[i][1] != 0)

    def halo_start(k, sides):
        for i in order:
            if DIRECTIONS[i][0] not in sides:
                continue

            @pl.when(exists(*DIRECTIONS[i]))
            def _():
                halo_copy(k, i).start()

    def halo_wait(k, which):
        for i in which:
            dy, dx = DIRECTIONS[i]

            @pl.when(exists(-dy, -dx))
            def _():
                halo_copy(k, i).wait_recv()

    halo_start(0, (-1, 0, 1))

    for i in range(8):
        dy, dx = DIRECTIONS[i]

        @pl.when(jnp.logical_not(exists(-dy, -dx)))
        def _():
            for k in range(layers):
                view = fields.at[k, landing(dy, H), landing(dx, W)]
                view[...] = jnp.zeros(view.shape, BF16)

    r_at = lax.broadcasted_iota(jnp.int32, (C, LANES), 0)
    l_at = lax.broadcasted_iota(jnp.int32, (C, LANES), 1)
    repeat = (l_at % C == r_at).astype(BF16)
    group = l_at // C

    def spread(w):
        return dot(w, repeat)

    for c in loads[1:]:
        c.wait()

    def plane_weights(l):
        for t in range(9):
            wide = spread(plane_taps[(l * 9 + t) * C : (l * 9 + t + 1) * C, :])
            for i in range(pack):
                at = t * LANES + i * C
                w_plane[l, at : at + C, :] = jnp.where(group == i, wide, 0.0).astype(BF16)

    bias_p = jnp.concatenate([plane_bias[...]] * pack, axis=1)
    bias_s = jnp.concatenate([shift_bias[...]] * pack, axis=1)
    bias_g = jnp.concatenate([gate_bias[...]] * pack, axis=1)
    gain = jnp.concatenate([gain_ref[...]] * pack, axis=1)

    def shift_weights(l):
        wides = [
            spread(shift_taps[(l * taps + t) * C : (l * taps + t + 1) * C, :]) for t in range(taps)
        ]
        for j in range(-reach, reach + 1):
            for i in range(pack):
                value = jnp.zeros((C, LANES), F32)
                for o in range(pack):
                    t = pack * j + i - o + half
                    if 0 <= t < taps:
                        value = jnp.where(group == o, wides[t], value)
                at = (j + reach) * LANES + i * C
                w_shift[l, at : at + C, :] = value.astype(BF16)

    def small_weights():
        a = lax.broadcasted_iota(jnp.int32, (3 * C, 3 * 128), 0)
        b = lax.broadcasted_iota(jnp.int32, (3 * C, 3 * 128), 1)
        place = jnp.logical_and(a // C == b // 128, a % C == b % 128).astype(BF16)
        wide = dot(qkv_ref[...], place).astype(BF16)
        w_qkv[...] = jnp.zeros(w_qkv.shape, BF16)
        for i in range(pack):
            w_qkv[i * C : (i + 1) * C, i * 384 : (i + 1) * 384] = wide
        w_exit[...] = jnp.zeros(w_exit.shape, BF16)
        wide = spread(exit_ref[...])
        for i in range(pack):
            w_exit[i * 128 : i * 128 + C, :] = jnp.where(group == i, wide, 0.0).astype(BF16)
        wide = spread(gate_ref[...])
        for i in range(pack):
            w_gate[i * C : (i + 1) * C, :] = jnp.where(group == i, wide, 0.0).astype(BF16)
        padded[:, 0:8, :] = jnp.zeros((W, 8, LANES), F32)
        padded[:, B + 8 : B + 16, :] = jnp.zeros((W, 8, LANES), F32)

    def there_copy(a, o):
        to = lax.rem(disp + o, nd)
        return pltpu.make_async_remote_copy(
            src_ref=slabs.at[a, to],
            dst_ref=lines.at[a, disp],
            send_sem=there_send.at[a, o - 1],
            recv_sem=there_recv.at[a, o - 1],
            device_id={"disp": to},
            device_id_type=MESH,
        )

    def plane_row(k, h, slot=None):
        lhs = jnp.concatenate(
            [
                fields[k, h + dy, dx : dx + W].reshape(W * bl, LANES)
                for dy in range(3)
                for dx in range(3)
            ],
            axis=1,
        )
        v = dot(lhs, w_plane[k]) + bias_p[k : k + 1]
        v = (v * sigmoid(v)).astype(BF16).reshape(W, bl, LANES)
        if k + 1 < layers:
            fields[k + 1, 1 + h, 1 : W + 1] = v
        else:
            slabs[slot] = v

    sides = [i for i in range(8) if DIRECTIONS[i][0] == 0]
    below = [i for i in range(8) if DIRECTIONS[i][0] == -1]
    above = [i for i in range(8) if DIRECTIONS[i][0] == 1]
    plane_weights(0)
    for k in range(layers - 1):
        halo_wait(k, sides)
        for h in range(1, H - 1):
            plane_row(k, h)
        plane_weights(k + 1)
        if k == 0:
            small_weights()
        if k == layers - 2:
            shift_weights(0)
        halo_wait(k, above)
        if H > 1:
            plane_row(k, 0)
            halo_start(k + 1, (-1,))
        halo_wait(k, below)
        plane_row(k, H - 1)
        halo_start(k + 1, (1, 0) if H > 1 else (-1, 1, 0))

    k = layers - 1
    halo_wait(k, sides)
    waited = False
    for a, rows_here in enumerate(stages):
        inner = [h for h in rows_here if 0 < h < H - 1]
        outer = [h for h in rows_here if not 0 < h < H - 1]
        if outer and not inner and not waited:
            shift_weights(1)
            halo_wait(k, above + below)
            waited = True
        if len(inner) == nd or len(outer) == nd == 2:
            for o in list(range(1, nd)) + [0]:
                q = lax.rem(disp + o, nd)
                h = 1 + a * nd + q if inner else q * (H - 1)
                plane_row(k, h, (a, q))
                if o:
                    there_copy(a, o).start()
        else:
            for h in inner:
                plane_row(k, h, (a, rows_here.index(h)))
            if outer and not waited:
                shift_weights(1)
                halo_wait(k, above + below)
                waited = True
            for h in outer:
                plane_row(k, h, (a, rows_here.index(h)))
            for o in range(1, nd):
                there_copy(a, o).start()
        lines[a, disp] = slabs[a, disp]

    def shift_conv(l, p0):
        lhs = jnp.concatenate(
            [
                padded[pl.ds(p0, step), 8 + j : 8 + j + B, :].astype(BF16).reshape(step * B, LANES)
                for j in range(-reach, reach + 1)
            ],
            axis=1,
        )
        return dot(lhs, w_shift[l]) + bias_s[l : l + 1]

    ones_a = lax.broadcasted_iota(jnp.int32, (LANES, LANES), 0) // C
    ones_b = lax.broadcasted_iota(jnp.int32, (LANES, LANES), 1) // C
    ones = (ones_a == ones_b).astype(BF16)

    def conv_chunk(p0):
        v = shift_conv(0, p0)
        v = (v * sigmoid(v)).astype(BF16).astype(F32)
        padded[pl.ds(p0, step), 8 : 8 + B, :] = v.reshape(step, B, LANES)
        v = shift_conv(1, p0).astype(BF16)
        second[pl.ds(p0, step)] = v.reshape(step, B, LANES)
        v = v.astype(F32)
        square = v * v
        high = square.astype(BF16)
        low = (square - high.astype(F32)).astype(BF16)
        mean = (dot(high, ones) + dot(low, ones)) * (1.0 / C)
        normed = (v * lax.rsqrt(mean + 1e-05) * gain).astype(BF16)
        joined[pl.ds(p0, step)] = dot(normed, w_qkv[...]).astype(BF16).reshape(step, B, pack * 384)

    D = pack * B
    hd = C // heads
    lane = lax.broadcasted_iota(jnp.int32, (D, 128), 1)
    together = LANES // D if heads % max(LANES // D, 1) == 0 else 1
    together = max(together, 1)
    factor = math.log2(math.e) / math.sqrt(hd)
    ones_rows = jnp.ones((16, D), BF16)
    scales = [
        jnp.concatenate(
            [
                jnp.broadcast_to(scale_ref[:, h : h + 1] * factor, (1, D))
                for h in range(g, g + together)
            ],
            axis=1,
        )
        for g in range(0, heads, together)
    ]

    def one_pixel(p):
        t = joined[p]
        q, k, v = (
            jnp.concatenate(
                [t[:, i * 384 + g * 128 : i * 384 + (g + 1) * 128] for i in range(pack)], axis=0
            )
            for g in range(3)
        )
        vt = v.astype(F32).T.astype(BF16)
        outs = []
        for n, g in enumerate(range(0, heads, together)):
            queries = jnp.concatenate(
                [
                    jnp.where(lane // hd == h, q, jnp.zeros_like(q))
                    for h in range(g, g + together)
                ],
                axis=0,
            )
            scores = lax.dot_general(
                k, queries, (((1,), (1,)), ((), ())), preferred_element_type=F32
            )
            top = jnp.max(scores, axis=0, keepdims=True)
            weights = jnp.exp2((scores - top) * scales[n]).astype(BF16)
            values = jnp.concatenate([vt[g * hd : (g + together) * hd], ones_rows], axis=0)
            o = dot(values, weights)
            inverse = 1.0 / o[together * hd : together * hd + 1]
            for i in range(together):
                cut = slice(i * D, (i + 1) * D)
                outs.append(o[i * hd : (i + 1) * hd, cut] * inverse[:, cut])
        o = jnp.concatenate(outs, axis=0)
        if C < 128:
            o = jnp.concatenate([o, jnp.zeros((128 - C, D), F32)], axis=0)
        o = o.T.astype(BF16)
        for i in range(pack):
            mixed[p, :, i * 128 : (i + 1) * 128] = o[i * B : (i + 1) * B]

    group_px = 4 if step % 4 == 0 else 1

    def back_copy(a, part, o):
        to = lax.rem(disp + o, nd)
        cut = pl.ds(part * step, step)
        return pltpu.make_async_remote_copy(
            src_ref=back.at[a, to, cut],
            dst_ref=returned.at[a, disp, cut],
            send_sem=back_send.at[a, part, o - 1],
            recv_sem=back_recv.at[a, part, o - 1],
            device_id={"disp": to},
            device_id_type=MESH,
        )

    def exit_chunk(a, p0):
        v = second[pl.ds(p0, step)].astype(F32).reshape(step * B, LANES)
        v = v + dot(mixed[pl.ds(p0, step)].reshape(step * B, pack * 128), w_exit[...])
        v = v.astype(BF16).reshape(step, B, LANES)
        for s in range(nd):
            back[a, s, pl.ds(p0, step)] = v[:, s * bl : (s + 1) * bl]
        returned[a, disp, pl.ds(p0, step)] = back[a, disp, pl.ds(p0, step)]

    for a in range(hr):
        for o in range(1, nd):
            there_copy(a, o).wait_recv()
        for s in range(nd):
            padded[:, 8 + s * bl : 8 + (s + 1) * bl, :] = lines[a, s].astype(F32)

        def one_part(part, carry):
            p0 = part * step
            conv_chunk(p0)

            def pixels(c, inner):
                for i in range(group_px):
                    one_pixel(p0 + c * group_px + i)
                return inner

            lax.fori_loop(0, step // group_px, pixels, 0)
            exit_chunk(a, p0)
            for o in range(1, nd):
                back_copy(a, part, o).start()
            return carry

        lax.fori_loop(0, parts, one_part, 0)

    for a, rows_here in enumerate(stages):
        for part in range(parts):
            for o in range(1, nd):
                back_copy(a, part, o).wait_recv()
            for n, h in enumerate(rows_here):
                w0 = part * step
                v = returned[a, n, w0 : w0 + step].reshape(step * bl, LANES)
                v = sigmoid(dot(v, w_gate[...]) + bias_g)
                x = fields[0, 1 + h, 1 + w0 : 1 + w0 + step].astype(F32)
                v = v * x.reshape(step * bl, LANES)
                at = (h * W + w0) * bl
                for s in range(2):
                    stage[s, at : at + step * bl, :] = v[:, s * 128 : (s + 1) * 128]
        for h in rows_here:
            for b in range(bl):
                for s in range(2):
                    out_ref[h, :, b * LANES + s * 128 : b * LANES + (s + 1) * 128] = stage[
                        s, pl.ds(h * W * bl + b, W, stride=bl), :
                    ].astype(BF16)

    for k in range(layers):
        for i in range(8):
            @pl.when(exists(*DIRECTIONS[i]))
            def _():
                halo_copy(k, i).wait_send()
    for o in range(1, nd):
        for a in range(hr):
            there_copy(a, o).wait_send()
            for part in range(parts):
                back_copy(a, part, o).wait_send()


def per_device(axes, x, ptaps, pbias, staps, sbias, gain, qkv, wexit, scale, gate, gbias):
    nr, nd, nc = axes
    H, W, flat = x.shape
    C = ptaps.shape[-1]
    layers, taps, heads = ptaps.shape[0], staps.shape[1], scale.shape[0]
    pack = LANES // C
    bl = flat // LANES
    B = nd * bl
    hr = H // nd
    parts = W // 8 if W % 8 == 0 else 1
    reach = (taps // 2 + pack - 1) // pack
    sizes = (nr, nd, nc, H, W, bl, C, layers, taps, heads)
    peers = max(nd - 1, 1)
    arguments = (
        x,
        ptaps.reshape(-1, C),
        pbias,
        staps.reshape(-1, C),
        sbias,
        gain.reshape(1, C),
        qkv,
        wexit,
        scale.reshape(1, heads),
        gate,
        gbias.reshape(1, C),
    )
    return pl.pallas_call(
        functools.partial(kernel, sizes),
        out_shape=jax.ShapeDtypeStruct(x.shape, x.dtype),
        in_specs=[pl.BlockSpec(memory_space=pltpu.HBM)] * len(arguments),
        out_specs=pl.BlockSpec(memory_space=pltpu.VMEM),
        scratch_shapes=[pltpu.VMEM(v.shape, v.dtype) for v in arguments]
        + [
            pltpu.VMEM((layers, H + 2, W + 2, bl, LANES), BF16),
            pltpu.VMEM((hr, nd, W, bl, LANES), BF16),
            pltpu.VMEM((hr, nd, W, bl, LANES), BF16),
            pltpu.VMEM((W, B + 16, LANES), F32),
            pltpu.VMEM((W, B, LANES), BF16),
            pltpu.VMEM((W, B, pack * 384), BF16),
            pltpu.VMEM((W, B, pack * 128), BF16),
            pltpu.VMEM((hr, nd, W, bl, LANES), BF16),
            pltpu.VMEM((hr, nd, W, bl, LANES), BF16),
            pltpu.VMEM((2, H * W * bl, 128), F32),
            pltpu.VMEM((layers, 9 * LANES, LANES), BF16),
            pltpu.VMEM((2, (2 * reach + 1) * LANES, LANES), BF16),
            pltpu.VMEM((LANES, pack * 384), BF16),
            pltpu.VMEM((pack * 128, LANES), BF16),
            pltpu.VMEM((LANES, LANES), BF16),
            pltpu.SemaphoreType.DMA((layers, 8)),
            pltpu.SemaphoreType.DMA((layers, 8)),
            pltpu.SemaphoreType.DMA((hr, peers)),
            pltpu.SemaphoreType.DMA((hr, peers)),
            pltpu.SemaphoreType.DMA((hr, parts, peers)),
            pltpu.SemaphoreType.DMA((hr, parts, peers)),
            pltpu.SemaphoreType.DMA((len(arguments),)),
        ],
        compiler_params=pltpu.CompilerParams(
            collective_id=0, has_side_effects=True, vmem_limit_bytes=48 * 1024 * 1024
        ),
    )(*arguments)


def solution(mesh):
    axes = tuple(mesh.shape[a] for a in ("rows", "disp", "cols"))
    spec = P(("groups", "rows"), "cols", "disp")
    return jax.shard_map(
        functools.partial(per_device, axes),
        mesh=mesh,
        in_specs=(spec,) + (P(),) * 10,
        out_specs=spec,
        check_vma=False,
    )
```

time: 59.1 us -> 52.2 us (0.88)
  Pallas kernels: 51.8 us -> 44.9 us
    pallas_call x1, Pallas kernels: 51.8 us -> 44.9 us  [per_device(): pl.pallas_call(functools.partial(kernel, sizes), out_shape=jax.ShapeDtype...]
where the time goes in v1:
time: 52.2 us; the launch traced here: 51.7 us
  Pallas kernels  44.9 us (86%)
  local copies, waits for them, and re-layouts  6.81 us (13%)
    pallas_call x1, Pallas kernels, per_device(): pl.pallas_call(functools.partial(kernel, sizes), out_shape=jax.ShapeDtype...  44.9 us
    unnamed x23, local copies, waits for them, and re-layouts  6.81 us

profile of v1, /device:TPU:0, one launch (start us, length us, event | category | flops | bytes accessed | tf_op | source)
XLA Modules:
  0.0 51.7 jit_solution(211028492501194961)
XLA Ops:
  0.0 0.0 copy-start.9
  0.0 0.0 copy-start.10
  0.0 0.0 copy-start.6
  0.0 0.0 copy-start.7
  0.0 0.0 copy-start.8
  0.0 0.6 %copy-done.9 = f32[4]{0:T(128)S(1)} copy-done((f32[4]{0:T(128)S(1)}, f32[4]{0:T(128)}, u32[]{:S(2)}) %copy-start.9) | copy-done | bytes 40
  0.7 0.0 copy-done.10
  0.7 0.0 copy-done.6
  0.7 0.0 copy-done.7
  0.7 0.0 copy-done.8
  0.7 0.0 copy-start
  0.7 1.1 %copy-done = bf16[2,17,64,64]{3,2,1,0:T(8,128)(2,1)S(1)} copy-done((bf16[2,17,64,64]{3,2,1,0:T(8,128)(2,1)S(1)}, bf16[2,17,64,64]{3,2,1,0:T(8,128)(2,1)}, u32[]{:S(2)}) %copy-start) | copy-done | bytes 278552
  1.8 0.0 copy-start.1
  1.8 1.0 %copy-done.1 = bf16[4,16,4096]{2,1,0:T(8,128)(2,1)S(1)} copy-done((bf16[4,16,4096]{2,1,0:T(8,128)(2,1)S(1)}, bf16[4,16,4096]{2,1,0:T(8,128)(2,1)}, u32[]{:S(2)}) %copy-start.1) | copy-done | bytes 524312
  2.8 0.0 copy-start.2
  2.8 1.0 %copy-done.2 = bf16[3,3,3,64,64]{4,3,2,1,0:T(8,128)(2,1)S(1)} copy-done((bf16[3,3,3,64,64]{4,3,2,1,0:T(8,128)(2,1)S(1)}, bf16[3,3,3,64,64]{4,3,2,1,0:T(8,128)(2,1)}, u32[]{:S(2)}) %copy-start.2) | copy-done | bytes 221208
  3.8 0.0 copy-start.3
  3.8 0.8 %copy-done.3 = bf16[64,192]{1,0:T(8,128)(2,1)S(1)} copy-done((bf16[64,192]{1,0:T(8,128)(2,1)S(1)}, bf16[64,192]{1,0:T(8,128)(2,1)}, u32[]{:S(2)}) %copy-start.3) | copy-done | bytes 24600
  4.6 0.0 copy-start.4
  4.6 0.7 %copy-done.4 = bf16[64,64]{1,0:T(8,128)(2,1)S(1)} copy-done((bf16[64,64]{1,0:T(8,128)(2,1)S(1)}, bf16[64,64]{1,0:T(8,128)(2,1)}, u32[]{:S(2)}) %copy-start.4) | copy-done | bytes 8216
  5.3 0.0 copy-start.5
  5.3 0.7 %copy-done.5 = bf16[64,64]{1,0:T(8,128)(2,1)S(1)} copy-done((bf16[64,64]{1,0:T(8,128)(2,1)S(1)}, bf16[64,64]{1,0:T(8,128)(2,1)}, u32[]{:S(2)}) %copy-start.5) | copy-done | bytes 8216
  6.0 44.9 %shard_map.109 = bf16[4,16,4096]{2,1,0:T(8,128)(2,1)S(1)} custom-call(bf16[4,16,4096]{2,1,0:T(8,128)(2,1)S(1)} %copy-done.1, bf16[1728,64]{1,0:T(8,128)(2,1)S(1)} %bitcast.6, f32[3,64]{1,0:T(4,128)S(1)} %copy-done.6, bf16[2176,64]{1,0:T(8,128)(2,1)S(1)} %bitcast.5, f32[2,64]{1,0:T(2,128)S(1)} %copy-done.7, f32[1,64]{1,0:T(1,128)S(1)} %bitcast.7, ...), custom_call_target="tpu_custom_call" | custom-call | tf_op jit(solution)/shard_map/pallas_call | solution.py:495
  50.9 0.8 %copy.13 = bf16[4,16,4096]{2,1,0:T(8,128)(2,1)} copy(bf16[4,16,4096]{2,1,0:T(8,128)(2,1)S(1)} %shard_map.109) | data formatting | bytes 1048576
Async XLA Ops:
  0.0 0.7 %copy-start.9 = (f32[4]{0:T(128)S(1)}, f32[4]{0:T(128)}, u32[]{:S(2)}) copy-start(f32[4]{0:T(128)} %param.19) | copy-start | bytes 52
  0.0 0.7 %copy-start.10 = (f32[64]{0:T(128)S(1)}, f32[64]{0:T(128)}, u32[]{:S(2)}) copy-start(f32[64]{0:T(128)} %param.21) | copy-start | bytes 772
  0.0 0.7 %copy-start.6 = (f32[3,64]{1,0:T(4,128)S(1)}, f32[3,64]{1,0:T(4,128)}, u32[]{:S(2)}) copy-start(f32[3,64]{1,0:T(4,128)} %refs_2_.1) | copy-start | bytes 2308
  0.0 0.7 %copy-start.7 = (f32[2,64]{1,0:T(2,128)S(1)}, f32[2,64]{1,0:T(2,128)}, u32[]{:S(2)}) copy-start(f32[2,64]{1,0:T(2,128)} %refs_4_.1) | copy-start | bytes 1540
  0.0 0.7 %copy-start.8 = (f32[64]{0:T(128)S(1)}, f32[64]{0:T(128)}, u32[]{:S(2)}) copy-start(f32[64]{0:T(128)} %param.16) | copy-start | bytes 772
  0.7 1.1 %copy-start = (bf16[2,17,64,64]{3,2,1,0:T(8,128)(2,1)S(1)}, bf16[2,17,64,64]{3,2,1,0:T(8,128)(2,1)}, u32[]{:S(2)}) copy-start(bf16[2,17,64,64]{3,2,1,0:T(8,128)(2,1)} %param.14) | copy-start | bytes 835588
  1.8 1.0 %copy-start.1 = (bf16[4,16,4096]{2,1,0:T(8,128)(2,1)S(1)}, bf16[4,16,4096]{2,1,0:T(8,128)(2,1)}, u32[]{:S(2)}) copy-start(bf16[4,16,4096]{2,1,0:T(8,128)(2,1)} %refs_0_.1) | copy-start | bytes 1572868
  2.8 1.0 %copy-start.2 = (bf16[3,3,3,64,64]{4,3,2,1,0:T(8,128)(2,1)S(1)}, bf16[3,3,3,64,64]{4,3,2,1,0:T(8,128)(2,1)}, u32[]{:S(2)}) copy-start(bf16[3,3,3,64,64]{4,3,2,1,0:T(8,128)(2,1)} %param.12) | copy-start | bytes 663556
  3.8 0.8 %copy-start.3 = (bf16[64,192]{1,0:T(8,128)(2,1)S(1)}, bf16[64,192]{1,0:T(8,128)(2,1)}, u32[]{:S(2)}) copy-start(bf16[64,192]{1,0:T(8,128)(2,1)} %refs_6_.1) | copy-start | bytes 73732
  4.6 0.7 %copy-start.4 = (bf16[64,64]{1,0:T(8,128)(2,1)S(1)}, bf16[64,64]{1,0:T(8,128)(2,1)}, u32[]{:S(2)}) copy-start(bf16[64,64]{1,0:T(8,128)(2,1)} %refs_7_.1) | copy-start | bytes 24580
  5.3 0.7 %copy-start.5 = (bf16[64,64]{1,0:T(8,128)(2,1)S(1)}, bf16[64,64]{1,0:T(8,128)(2,1)}, u32[]{:S(2)}) copy-start(bf16[64,64]{1,0:T(8,128)(2,1)} %refs_9_.1) | copy-start | bytes 24580

commit v2 on v1

--- a/solution.py
+++ b/solution.py
@@ -240,21 +240,24 @@
             device_id_type=MESH,
         )
 
-    def plane_row(k, h, slot=None):
+    def plane_rows(k, h, n):
         lhs = jnp.concatenate(
             [
-                fields[k, h + dy, dx : dx + W].reshape(W * bl, LANES)
+                fields[k, pl.ds(h + dy, n), dx : dx + W].reshape(n * W * bl, LANES)
                 for dy in range(3)
                 for dx in range(3)
             ],
             axis=1,
         )
         v = dot(lhs, w_plane[k]) + bias_p[k : k + 1]
-        v = (v * sigmoid(v)).astype(BF16).reshape(W, bl, LANES)
+        return (v * sigmoid(v)).astype(BF16).reshape(n, W, bl, LANES)
+
+    def plane_row(k, h, slot=None, n=1):
+        v = plane_rows(k, h, n)
         if k + 1 < layers:
-            fields[k + 1, 1 + h, 1 : W + 1] = v
+            fields[k + 1, 1 + h : 1 + h + n, 1 : W + 1] = v
         else:
-            slabs[slot] = v
+            slabs[slot] = v[0]
 
     sides = [i for i in range(8) if DIRECTIONS[i][0] == 0]
     below = [i for i in range(8) if DIRECTIONS[i][0] == -1]
@@ -262,8 +265,8 @@
     plane_weights(0)
     for k in range(layers - 1):
         halo_wait(k, sides)
-        for h in range(1, H - 1):
-            plane_row(k, h)
+        if H > 2:
+            plane_row(k, 1, n=H - 2)
         plane_weights(k + 1)
         if k == 0:
             small_weights()
@@ -287,7 +290,13 @@
             shift_weights(1)
             halo_wait(k, above + below)
             waited = True
-        if len(inner) == nd or len(outer) == nd == 2:
+        if len(inner) == nd == H - 2:
+            v = plane_rows(k, 1, nd)
+            for n in range(nd):
+                slabs[a, n] = v[n]
+            for o in range(1, nd):
+                there_copy(a, o).start()
+        elif len(inner) == nd or len(outer) == nd == 2:
             for o in list(range(1, nd)) + [0]:
                 q = lax.rem(disp + o, nd)
                 h = 1 + a * nd + q if inner else q * (H - 1)
@@ -307,10 +316,10 @@
                 there_copy(a, o).start()
         lines[a, disp] = slabs[a, disp]
 
-    def shift_conv(l, p0):
+    def shift_conv(l):
         lhs = jnp.concatenate(
             [
-                padded[pl.ds(p0, step), 8 + j : 8 + j + B, :].astype(BF16).reshape(step * B, LANES)
+                padded[:, 8 + j : 8 + j + B, :].astype(BF16).reshape(W * B, LANES)
                 for j in range(-reach, reach + 1)
             ],
             axis=1,
@@ -321,19 +330,19 @@
     ones_b = lax.broadcasted_iota(jnp.int32, (LANES, LANES), 1) // C
     ones = (ones_a == ones_b).astype(BF16)
 
-    def conv_chunk(p0):
-        v = shift_conv(0, p0)
+    def conv_rows():
+        v = shift_conv(0)
         v = (v * sigmoid(v)).astype(BF16).astype(F32)
-        padded[pl.ds(p0, step), 8 : 8 + B, :] = v.reshape(step, B, LANES)
-        v = shift_conv(1, p0).astype(BF16)
-        second[pl.ds(p0, step)] = v.reshape(step, B, LANES)
+        padded[:, 8 : 8 + B, :] = v.reshape(W, B, LANES)
+        v = shift_conv(1).astype(BF16)
+        second[...] = v.reshape(W, B, LANES)
         v = v.astype(F32)
         square = v * v
         high = square.astype(BF16)
         low = (square - high.astype(F32)).astype(BF16)
         mean = (dot(high, ones) + dot(low, ones)) * (1.0 / C)
         normed = (v * lax.rsqrt(mean + 1e-05) * gain).astype(BF16)
-        joined[pl.ds(p0, step)] = dot(normed, w_qkv[...]).astype(BF16).reshape(step, B, pack * 384)
+        joined[...] = dot(normed, w_qkv[...]).astype(BF16).reshape(W, B, pack * 384)
 
     D = pack * B
     hd = C // heads
@@ -389,7 +398,7 @@
         for i in range(pack):
             mixed[p, :, i * 128 : (i + 1) * 128] = o[i * B : (i + 1) * B]
 
-    group_px = 4 if step % 4 == 0 else 1
+    group_px = 8 if step % 8 == 0 else 1
 
     def back_copy(a, part, o):
         to = lax.rem(disp + o, nd)
@@ -417,9 +426,10 @@
         for s in range(nd):
             padded[:, 8 + s * bl : 8 + (s + 1) * bl, :] = lines[a, s].astype(F32)
 
+        conv_rows()
+
         def one_part(part, carry):
             p0 = part * step
-            conv_chunk(p0)
 
             def pixels(c, inner):
                 for i in range(group_px):
@@ -523,7 +533,7 @@
             pltpu.SemaphoreType.DMA((len(arguments),)),
         ],
         compiler_params=pltpu.CompilerParams(
-            collective_id=0, has_side_effects=True, vmem_limit_bytes=48 * 1024 * 1024
+            collective_id=0, has_side_effects=True, vmem_limit_bytes=63 * 1024 * 1024
         ),
     )(*arguments)
 

time: 52.2 us -> 44.4 us (0.85)
  local copies, waits for them, and re-layouts: 6.81 us -> 1.87 us
  Pallas kernels: 44.9 us -> 42.3 us
    unnamed x23 -> x1, local copies, waits for them, and re-layouts: 6.81 us -> 1.87 us
    pallas_call x1, Pallas kernels: 44.9 us -> 42.3 us  [per_device(): pl.pallas_call(functools.partial(kernel, sizes), out_shape=jax.ShapeDtype...]
where the time goes in v2:
time: 44.4 us; the launch traced here: 44.2 us
  Pallas kernels  42.3 us (95%)
  local copies, waits for them, and re-layouts  1.87 us (4%)
    pallas_call x1, Pallas kernels, per_device(): pl.pallas_call(functools.partial(kernel, sizes), out_shape=jax.ShapeDtype...  42.3 us
    unnamed x1, local copies, waits for them, and re-layouts  1.87 us

profile of v2, /device:TPU:0, one launch (start us, length us, event | category | flops | bytes accessed | tf_op | source)
XLA Modules:
  0.0 44.2 jit_solution(3640914941322219021)
XLA Ops:
  0.0 42.3 %shard_map.109 = bf16[4,16,4096]{2,1,0:T(8,128)(2,1)} custom-call(bf16[4,16,4096]{2,1,0:T(8,128)(2,1)} %refs_0_.1, bf16[1728,64]{1,0:T(8,128)(2,1)} %bitcast.6, f32[3,64]{1,0:T(4,128)} %refs_2_.1, bf16[2176,64]{1,0:T(8,128)(2,1)} %bitcast.5, f32[2,64]{1,0:T(2,128)} %refs_4_.1, f32[1,64]{1,0:T(1,128)} %bitcast.7, bf16[64,192]{1,0:T(8,128)(2,1)} %refs_6_.1, ...), custom_call_target="tpu_custom_call" | custom-call | tf_op jit(solution)/shard_map/pallas_call | solution.py:505
  42.4 1.9 %copy.13 = bf16[4,16,4096]{2,1,0:T(8,128)(2,1)} copy(bf16[4,16,4096]{2,1,0:T(8,128)(2,1)} %shard_map.109) | data formatting | bytes 1048576

commit v3 on v2

--- a/solution.py
+++ b/solution.py
@@ -452,8 +452,6 @@
                 w0 = part * step
                 v = returned[a, n, w0 : w0 + step].reshape(step * bl, LANES)
                 v = sigmoid(dot(v, w_gate[...]) + bias_g)
-                x = fields[0, 1 + h, 1 + w0 : 1 + w0 + step].astype(F32)
-                v = v * x.reshape(step * bl, LANES)
                 at = (h * W + w0) * bl
                 for s in range(2):
                     stage[s, at : at + step * bl, :] = v[:, s * 128 : (s + 1) * 128]
@@ -462,7 +460,7 @@
                 for s in range(2):
                     out_ref[h, :, b * LANES + s * 128 : b * LANES + (s + 1) * 128] = stage[
                         s, pl.ds(h * W * bl + b, W, stride=bl), :
-                    ].astype(BF16)
+                    ]
 
     for k in range(layers):
         for i in range(8):
@@ -502,9 +500,9 @@
         gate,
         gbias.reshape(1, C),
     )
-    return pl.pallas_call(
+    gate = pl.pallas_call(
         functools.partial(kernel, sizes),
-        out_shape=jax.ShapeDtypeStruct(x.shape, x.dtype),
+        out_shape=jax.ShapeDtypeStruct(x.shape, F32),
         in_specs=[pl.BlockSpec(memory_space=pltpu.HBM)] * len(arguments),
         out_specs=pl.BlockSpec(memory_space=pltpu.VMEM),
         scratch_shapes=[pltpu.VMEM(v.shape, v.dtype) for v in arguments]
@@ -536,6 +534,7 @@
             collective_id=0, has_side_effects=True, vmem_limit_bytes=63 * 1024 * 1024
         ),
     )(*arguments)
+    return (x.astype(F32) * gate).astype(x.dtype)
 
 
 def solution(mesh):

time: 44.4 us -> 44.8 us (level)
  other arithmetic: 0 us -> 2.11 us
  local copies, waits for them, and re-layouts: 1.87 us -> 0.01 us
    convert_element_type x0 -> x1, other arithmetic: none -> 2.11 us  [per_device(): return (x.astype(F32) * gate).astype(x.dtype)]
    unnamed x1 -> x2, local copies, waits for them, and re-layouts: 1.87 us -> 0.01 us
where the time goes in v3:
time: 44.8 us; the launch traced here: 44.6 us
  Pallas kernels  42.5 us (95%)
  other arithmetic  2.11 us (5%)
    pallas_call x1, Pallas kernels, per_device(): pl.pallas_call(functools.partial(kernel, sizes), out_shape=jax.ShapeDtype...  42.5 us
    convert_element_type x1, other arithmetic, per_device(): return (x.astype(F32) * gate).astype(x.dtype)  2.11 us

profile of v3, /device:TPU:0, one launch (start us, length us, event | category | flops | bytes accessed | tf_op | source)
XLA Modules:
  0.0 44.6 jit_solution(268717355819678329)
XLA Ops:
  0.0 0.0 copy-start
  0.0 42.5 %shard_map.109 = f32[4,16,4096]{2,1,0:T(8,128)} custom-call(bf16[4,16,4096]{2,1,0:T(8,128)(2,1)} %refs_0_.1, bf16[1728,64]{1,0:T(8,128)(2,1)} %bitcast.6, f32[3,64]{1,0:T(4,128)} %refs_2_.1, bf16[2176,64]{1,0:T(8,128)(2,1)} %bitcast.5, f32[2,64]{1,0:T(2,128)} %refs_4_.1, f32[1,64]{1,0:T(1,128)} %bitcast.7, bf16[64,192]{1,0:T(8,128)(2,1)} %refs_6_.1, ...), custom_call_target="tpu_custom_call" | custom-call | tf_op jit(solution)/shard_map/pallas_call | solution.py:503
  42.5 0.0 copy-done
  42.5 2.1 %multiply_convert_fusion = bf16[4,16,4096]{2,1,0:T(8,128)(2,1)} fusion(f32[4,16,4096]{2,1,0:T(8,128)} %shard_map.109, bf16[4,16,4096]{2,1,0:T(8,128)(2,1)S(1)} %copy-done), kind=kLoop, calls=%fused_computation | loop fusion | flops 786432 | bytes 2097152 | tf_op jit(solution)/shard_map/convert_element_type | solution.py:537
Async XLA Ops:
  0.0 42.5 %copy-start = (bf16[4,16,4096]{2,1,0:T(8,128)(2,1)S(1)}, bf16[4,16,4096]{2,1,0:T(8,128)(2,1)}, u32[]{:S(2)}) copy-start(bf16[4,16,4096]{2,1,0:T(8,128)(2,1)} %refs_0_.1) | copy-start | bytes 1572868
